TPU v7x, 32 devices: a whole 2x2x4 slice. The times are simulated.
32 devices in a mesh: dp: 2 (over y), tensor: 16 (over z, x, core).
Axes of the slice: x: 2, y: 2, z: 4, core: 2. Of those that a mesh axis runs over, the one named last changes fastest.
Arguments:
- hidden: bfloat16 [16, 256, 1536], P('dp', 'tensor'), may hold values from -24 to 24
- norm_gain: float32 [1536], replicated, may hold values from 0.1 to 1.9
- embedding: bfloat16 [49664, 1536], P('tensor'), may hold values from -2 to 2
- targets: int32 [16, 256], P('dp', 'tensor'), may hold values from 0 to 49154
- lengths: int32 [16], replicated, may hold values from 1 to 256, 2560 in all
- loss_mask: int32 [16, 256], P('dp', 'tensor'), may hold values 0 or 1
- deal_slots: int32 [16], replicated, may hold values from 0 to 15, as said below
Outputs:
- log_prob: float32 [16, 256], P('dp', 'tensor')
- entropy: float32 [16, 256], P('dp', 'tensor')
Inputs may be any that keep to these rules, and one draw needn't show every extreme that they name: A permutation; sequence k lies in data group deal_slots[k] // 8, and each data group's sequences go in equal numbers to every data group.
All inputs are finite; a program needn't handle non-finite values. No bound on the sum of `loss_mask` on one device may be relied on, other than what follows from the above.
Results may differ from a plain program's by a relative error of at most 0.012.
The roundings to bfloat16 on the way count: a program that leaves them out, or rounds other values in their place, can miss the bound.
Values may be sent and summed in bfloat16 or wider, within the bound.
A program may use at most 128 MiB of HBM per device.

v0:
```python
import jax
import jax.numpy as jnp
from jax import lax
from jax.sharding import PartitionSpec as P

VREAL = 49155


def normalize(hidden, norm_gain):
    values = hidden.astype(jnp.float32)
    inverse = lax.rsqrt(jnp.mean(values * values, axis=2, keepdims=True) + 1e-05)
    return (values * inverse * norm_gain).astype(jnp.bfloat16)


def score(normed, marked, embedding):
    sequences, row_width = marked.shape
    vocab_rows = embedding.shape[0]
    tensor_rank = lax.axis_index("tensor")
    columns = tensor_rank * vocab_rows + jnp.arange(vocab_rows, dtype=jnp.int32)
    usable = columns < VREAL
    row_block = lax.all_gather(normed, "tensor", axis=1, tiled=True)
    block_marks = lax.all_gather(marked, "tensor", axis=1, tiled=True)
    row_count = row_block.shape[1]
    flat_rows = row_block.reshape(sequences * row_count, row_block.shape[2])
    logits = jnp.einsum("nd,vd->nv", flat_rows, embedding, preferred_element_type=jnp.float32)
    maximum = jnp.max(jnp.where(usable, logits, -jnp.inf), axis=1)
    weights = jnp.where(usable, jnp.exp(logits - maximum[:, None]), 0.0)
    totals = jnp.sum(weights, axis=1)
    weighted = jnp.sum(weights * jnp.where(usable, logits, 0.0), axis=1)
    chosen = jnp.sum(
        jnp.where(columns[None, :] == block_marks.reshape(-1)[:, None], logits, 0.0), axis=1
    )
    fresh_stats = (maximum, totals, weighted, chosen)
    maximum, totals, weighted, chosen = tuple(
        (updated.reshape(sequences, row_count) for updated in fresh_stats)
    )
    own_start = tensor_rank * row_width
    overall = lax.pmax(maximum, "tensor")
    factor = jnp.exp(maximum - overall)
    summed = lax.psum((totals * factor, weighted * factor, chosen), "tensor")
    totals, weighted, chosen = [
        lax.dynamic_slice_in_dim(member, own_start, row_width, 1) for member in summed
    ]
    maximum = lax.dynamic_slice_in_dim(overall, own_start, row_width, 1)
    log_total = maximum + jnp.log(totals)
    usable_rows = marked >= 0
    return (
        jnp.where(usable_rows, chosen - log_total, 0.0),
        jnp.where(usable_rows, log_total - weighted / totals, 0.0),
    )


def local(hidden, norm_gain, embedding, targets, lengths, loss_mask, deal_slots):
    group_rank = lax.axis_index("dp")
    sequences = hidden.shape[0]
    row_width = hidden.shape[1]
    tensor_rank = lax.axis_index("tensor")
    owned_seqs = group_rank * sequences + jnp.arange(sequences, dtype=jnp.int32)
    destination = deal_slots[owned_seqs] // sequences
    send_order = jnp.argsort(destination, stable=True)
    every_group = deal_slots // sequences
    arrived = jnp.argsort((every_group != group_rank).astype(jnp.int32), stable=True)[:sequences]
    arrived_slot = deal_slots[arrived] % sequences
    positions = tensor_rank * row_width + jnp.arange(row_width, dtype=jnp.int32)
    scored = (positions[None, :] < lengths[owned_seqs][:, None]) & (loss_mask == 1)
    marked = jnp.where(scored, targets, -1)
    normed = normalize(hidden, norm_gain)
    undo_order = jnp.argsort(send_order)
    came = lax.all_to_all(marked[send_order], "dp", split_axis=0, concat_axis=0, tiled=True)
    worker_marks = came[jnp.argsort(arrived_slot)]
    log_prob, entropy = score(normed, worker_marks, embedding)
    returned = (
        lax.all_to_all(log_prob[arrived_slot], "dp", split_axis=0, concat_axis=0, tiled=True),
        lax.all_to_all(entropy[arrived_slot], "dp", split_axis=0, concat_axis=0, tiled=True),
    )
    return (returned[0][undo_order], returned[1][undo_order])


def solution(mesh):
    placed = (
        P("dp", "tensor", None),
        P(),
        P("tensor", None),
        P("dp", "tensor"),
        P(),
        P("dp", "tensor"),
        P(),
    )
    return jax.shard_map(
        local,
        mesh=mesh,
        in_specs=placed,
        out_specs=(P("dp", "tensor"), P("dp", "tensor")),
        check_vma=False,
    )
```

profile of v0, /device:TPU:0, one launch (start us, length us, event | category | flops | bytes accessed | tf_op | source)
XLA Modules:
  0.0 229.7 jit_solution(12281780831424158666)
XLA Ops:
  7.2 0.0 copy-start
  7.2 0.0 all-gather.4.cloned.1.call-start
  7.2 1.1 fusion.1
  8.4 1.9 fusion.3
  10.3 0.0 all-gather.4.cloned.1.call-update
  10.3 0.0 copy-done
  10.4 0.6 gather_fusion
  11.0 1.3 gather_fusion.1
  12.3 0.7 compare_convert_fusion
  13.0 1.2 sort.66
  14.2 1.0 sort.65
  15.2 0.8 and_select_fusion
  16.0 1.1 gather_fusion.2
  17.1 4.2 %all-to-all-start = ((s32[2,4,16]{2,1,0:T(4,128)}), s32[2,4,16]{2,1,0:T(4,128)S(1)}, u32[]{:S(2)}, u32[]{:S(2)}) async-start(s32[2,4,16]{2,1,0:T(4,128)} %bitcast.1), calls=%async_computation | async-start | bytes 8192 | tf_op jit(solution)/shard_map/all_to_all | solution.py:69
  21.4 1.3 gather_fusion.3
  22.7 1.0 sort.67
  23.7 1.0 sort.68
  24.7 0.5 all-to-all-done
  25.2 0.6 gather_fusion.4
  25.7 22.5 %all-gather.1 = s32[16,16,8]{1,2,0:T(8,128)S(1)} all-gather(s32[1,16,8]{1,2,0:T(8,128)S(1)} %bitcast.26), channel_id=2, replica_groups=mesh['dp'=2,'tensor'=16] {'tensor'}, dimensions={0}, use_global_device_ids=true | all-gather | bytes 8704 | tf_op jit(solution)/shard_map/all_gather | solution.py:22
  48.2 0.1 reshape.191
  48.3 26.9 %all-gather.4.cloned.1.call-done = bf16[8,256,1536]{2,1,0:T(8,128)(2,1)} async-done(((bf16[8,16,1536]{2,1,0:T(8,128)(2,1)}), bf16[8,256,1536]{2,1,0:T(8,128)(2,1)}) %all-gather.4.cloned.1.call-update) | async-done | bytes 6291472 | tf_op jit(solution)/shard_map/all_gather | solution.py:21
  75.2 26.9 %select_reduce_fusion = (f32[2048]{0:T(1024)S(1)}, f32[2048,3104]{0,1:T(8,128)}) fusion(pred[3104]{0:T(1024)(128)(4,1)S(1)} %broadcast_compare_fusion, bf16[2048,1536]{1,0:T(8,128)(2,1)} %bitcast.29, bf16[3104,1536]{1,0:T(8,128)(2,1)} %param.9), kind=kOutput, calls=%fused_computation.12 | convolution fusion | flops 19541391360 | bytes 41266208 | tf_op jit(solution)/shard_map/nd,vd->nv/dot_general | solution.py:25
  102.1 14.8 %multiply_reduce_fusion = (f32[2048]{0:T(1024)S(1)}, f32[2048]{0:T(1024)S(1)}, f32[2048]{0:T(1024)S(1)}) fusion(f32[2048,3104]{0,1:T(8,128)} %get-tuple-element.21, f32[2048]{0:T(1024)S(1)} %get-tuple-element.20, pred[3104]{0:T(1024)(128)(4,1)S(1)} %broadcast_compare_fusion, s32[2048]{0:T(1024)S(1)} %bitcast.27, s32[3104]{0:T(1024)S(1)} %iota_add_fusion), kind=kLoop, calls=%fused_computation.9 | loop fusion | flops 57206784 | bytes 25484448 | tf_op jit(solution)/shard_map/reduce_sum | solution.py:29
  116.9 31.8 %pmax.7 = f32[8,256]{1,0:T(8,128)S(1)} all-reduce(f32[8,256]{1,0:T(8,128)S(1)} %reshape.109), channel_id=1, replica_groups=mesh['dp'=2,'tensor'=16] {'tensor'}, use_global_device_ids=true, to_apply=%region_7.8 | all-reduce | flops 2048 | bytes 16384 | tf_op jit(solution)/shard_map/pmax | solution.py:38
  148.8 57.6 %all-reduce = (f32[8,256]{1,0:T(8,128)S(1)}, f32[8,256]{1,0:T(8,128)S(1)}, f32[8,256]{1,0:T(8,128)S(1)}) all-reduce(f32[8,256]{1,0:T(8,128)S(1)} %reshape.108, f32[8,256]{1,0:T(8,128)S(1)} %get-tuple-element.19, f32[8,256]{1,0:T(8,128)S(1)} %get-tuple-element.18), channel_id=1, replica_groups=mesh['dp'=2,'tensor'=16] {'tensor'}, use_global_device_ids=true, to_apply=%region_5.6 | all-reduce | flops 6144 | bytes 49152 | tf_op jit(solution)/shard_map/psum | solution.py:40
  206.4 0.1 subtract_select_fusion
  206.5 0.1 subtract_select_fusion.1
  206.6 1.1 gather_fusion.5
  207.7 3.2 %all-to-all-start.1 = ((f32[2,4,16]{2,1,0:T(4,128)}), f32[2,4,16]{2,1,0:T(4,128)S(1)}, u32[]{:S(2)}, u32[]{:S(2)}) async-start(f32[2,4,16]{2,1,0:T(4,128)} %bitcast.9), calls=%async_computation.1 | async-start | bytes 8192 | tf_op jit(solution)/shard_map/all_to_all | solution.py:73
  211.0 1.1 gather_fusion.7
  212.1 2.6 %all-to-all-done.1 = f32[2,4,16]{2,1,0:T(4,128)S(1)} async-done(((f32[2,4,16]{2,1,0:T(4,128)}), f32[2,4,16]{2,1,0:T(4,128)S(1)}, u32[]{:S(2)}, u32[]{:S(2)}) %all-to-all-start.1) | async-done | bytes 544 | tf_op jit(solution)/shard_map/all_to_all | solution.py:73
  214.7 3.2 %all-to-all-start.2 = ((f32[2,4,16]{2,1,0:T(4,128)}), f32[2,4,16]{2,1,0:T(4,128)S(1)}, u32[]{:S(2)}, u32[]{:S(2)}) async-start(f32[2,4,16]{2,1,0:T(4,128)} %bitcast.11), calls=%async_computation.2 | async-start | bytes 8192 | tf_op jit(solution)/shard_map/all_to_all | solution.py:74
  218.0 1.1 gather_fusion.6
  219.1 2.6 %all-to-all-done.2 = f32[2,4,16]{2,1,0:T(4,128)S(1)} async-done(((f32[2,4,16]{2,1,0:T(4,128)}), f32[2,4,16]{2,1,0:T(4,128)S(1)}, u32[]{:S(2)}, u32[]{:S(2)}) %all-to-all-start.2) | async-done | bytes 544 | tf_op jit(solution)/shard_map/all_to_all | solution.py:74
  221.8 1.1 gather_fusion.8
  (28 shorter events, 0.2 us)
Async XLA Ops:
  7.2 3.2 %copy-start = (s32[16]{0:T(128)S(1)}, s32[16]{0:T(128)}, u32[]{:S(2)}) copy-start(s32[16]{0:T(128)} %param.11) | copy-start | bytes 196
  7.2 68.0 %all-gather.4.cloned.1.call-start = ((), (), s32[]{:S(2)}) async-start(), calls=%async_computation.3 | async-start | bytes 6684672 | tf_op jit(solution)/shard_map/all_gather | solution.py:21
  17.1 8.0 %all-to-all-start = ((s32[2,4,16]{2,1,0:T(4,128)}), s32[2,4,16]{2,1,0:T(4,128)S(1)}, u32[]{:S(2)}, u32[]{:S(2)}) async-start(s32[2,4,16]{2,1,0:T(4,128)} %bitcast.1), calls=%async_computation | async-start | bytes 8192 | tf_op jit(solution)/shard_map/all_to_all | solution.py:69
  207.7 7.0 %all-to-all-start.1 = ((f32[2,4,16]{2,1,0:T(4,128)}), f32[2,4,16]{2,1,0:T(4,128)S(1)}, u32[]{:S(2)}, u32[]{:S(2)}) async-start(f32[2,4,16]{2,1,0:T(4,128)} %bitcast.9), calls=%async_computation.1 | async-start | bytes 8192 | tf_op jit(solution)/shard_map/all_to_all | solution.py:73
  214.7 7.0 %all-to-all-start.2 = ((f32[2,4,16]{2,1,0:T(4,128)}), f32[2,4,16]{2,1,0:T(4,128)S(1)}, u32[]{:S(2)}, u32[]{:S(2)}) async-start(f32[2,4,16]{2,1,0:T(4,128)} %bitcast.11), calls=%async_computation.2 | async-start | bytes 8192 | tf_op jit(solution)/shard_map/all_to_all | solution.py:74
Sparse Core Ops, SparseCore 0:
  10.4 64.7 all-gather.3
where the time goes:
time: 230 us
  blocking collectives  112 us (49%)
  waiting for transfers between devices  32.6 us (14%)
  matrix products  26.9 us (12%)
  other arithmetic  23.7 us (10%)
  between operations  14.2 us (6%)
  starting transfers between devices  10.7 us (5%)
  local copies, waits for them, and re-layouts  9.65 us (4%)
    psum x1, blocking collectives, score(): summed = lax.psum((totals * factor, weighted * factor, chosen), 'tensor')  57.6 us
    pmax x1, blocking collectives, score(): overall = lax.pmax(maximum, 'tensor')  31.8 us
    dot_general x1, matrix products, score(): jnp.einsum('nd,vd->nv', flat_rows, embedding, preferred_element_type=jnp....  26.9 us
    all_gather x1, waiting for transfers between devices, score(): row_block = lax.all_gather(normed, 'tensor', axis=1, tiled=True)  26.9 us
    all_gather x1, blocking collectives, score(): block_marks = lax.all_gather(marked, 'tensor', axis=1, tiled=True)  22.5 us
    reduce_sum x1, other arithmetic, score(): weighted = jnp.sum(weights * jnp.where(usable, logits, 0.0), axis=1)  14.8 us
  transfers between devices with their start and end apart: 4, of which 4 were waited for; matrix products, arithmetic and copies ran while one was open for 6% of the time, Pallas kernels for 0%

commit v1 on v0

v1 whole, which is shorter than its diff:
```python
import functools

import jax
import jax.numpy as jnp
from jax import lax
from jax.experimental import pallas as pl
from jax.experimental.pallas import tpu as pltpu
from jax.sharding import PartitionSpec as P

VREAL = 49155
MESH = pl.DeviceIdType.MESH


def vocab_tiles(total, want):
    units = -(-total // 16)
    parts = max(1, -(-total // want))
    starts = [16 * (units * i // parts) for i in range(parts)] + [total]
    return [(a, b - a) for a, b in zip(starts[:-1], starts[1:])]


def kernel(
    groups, n, seqs, tiles, low_valid,
    hidden_ref, gain_ref, table_hbm, wanted_ref, order_ref, out_ref,
    rows_buf, table, ids, fresh, stats,
    table_sem, ids_send, ids_recv, right_send, left_send, sib_send, recv, half_recv,
    stat_send, stat_recv,
):
    ring = n // 2
    last = ring // 2
    rows = hidden_ref.shape[0]
    half = rows // 2
    width = rows // seqs
    vocab = table_hbm.shape[0]
    everyone = groups * n
    g = lax.axis_index("dp")
    r = lax.axis_index("tensor")
    c = lax.rem(r, 2)

    def ring_of(rank):
        pair = rank // 2
        z, x = pair // 2, lax.rem(pair, 2)
        return z + x * (ring - 1 - 2 * z)

    def rank_of(place, core):
        x = place // last
        z = place + x * (ring - 1 - 2 * place)
        return 2 * (2 * z + x) + core

    q = ring_of(r)
    right = rank_of(lax.rem(q + 1, ring), c)
    left = rank_of(lax.rem(q + ring - 1, ring), c)
    sibling = rank_of(q, 1 - c)

    load = pltpu.make_async_copy(table_hbm, table, table_sem)
    load.start()

    barrier = pltpu.get_barrier_semaphore()

    def peer(k):
        return {"dp": lax.rem(g + k // n, groups), "tensor": lax.rem(r + lax.rem(k, n), n)}

    def greet(k, carry):
        pl.semaphore_signal(barrier, inc=1, device_id=peer(k), device_id_type=MESH)
        return carry

    lax.fori_loop(1, everyone, greet, 0)

    values = hidden_ref[...].astype(jnp.float32)
    inverse = lax.rsqrt(jnp.mean(values * values, axis=1, keepdims=True) + 1e-05)
    rows_buf[q, c] = (values * inverse * gain_ref[...]).astype(jnp.bfloat16)
    ids[0] = wanted_ref[...]

    pl.semaphore_wait(barrier, everyone - 1)

    def chunk_copy(place, core, send_sem, recv_sem, to, part=None):
        ref = rows_buf.at[place, core]
        if part is not None:
            ref = rows_buf.at[place, core, pl.ds(part * half, half)]
        return pltpu.make_async_remote_copy(
            src_ref=ref, dst_ref=ref, send_sem=send_sem, recv_sem=recv_sem,
            device_id={"dp": g, "tensor": to}, device_id_type=MESH,
        )

    chunk_copy(q, c, right_send.at[0], recv.at[q, c], right).start()
    chunk_copy(q, c, left_send.at[0], recv.at[q, c], left).start()
    chunk_copy(q, c, sib_send.at[0], recv.at[q, c], sibling).start()

    def ids_copy(k):
        return pltpu.make_async_remote_copy(
            src_ref=wanted_ref, dst_ref=ids.at[k], send_sem=ids_send.at[k], recv_sem=ids_recv,
            device_id=peer(k), device_id_type=MESH,
        )

    def send_ids(k, carry):
        ids_copy(k).start()
        return carry

    lax.fori_loop(1, everyone, send_ids, 0)
    others = pl.ds(1, everyone - 1)
    pltpu.make_async_remote_copy(
        src_ref=ids.at[others], dst_ref=ids.at[others], send_sem=ids_send.at[0],
        recv_sem=ids_recv, device_id=peer(1), device_id_type=MESH,
    ).wait_recv()
    load.wait()

    segment = lax.broadcasted_iota(jnp.int32, (1, rows), 1) // width

    def wanted_of(rank):
        line = jnp.zeros((1, rows), jnp.int32)
        for s in range(seqs):
            seq = order_ref[s]
            back = lax.rem(g - seq // seqs + groups, groups)
            where = back * n + lax.rem(r - rank + n, n)
            line = jnp.where(segment == s, ids[where, pl.ds(lax.rem(seq, seqs), 1), :], line)
        return line

    def stat_copy(k, place, core, j):
        rank = rank_of(place, core)
        slot = j * n + lax.rem(rank - r + n, n)
        return pltpu.make_async_remote_copy(
            src_ref=fresh.at[place, core], dst_ref=stats.at[slot],
            send_sem=stat_send.at[k, core, j], recv_sem=stat_recv,
            device_id={"dp": lax.rem(g + j, groups), "tensor": rank}, device_id_type=MESH,
        )

    def block(b, carry):
        step = (b + 1) // 2
        side = lax.rem(b + 1, 2)
        came_l = lax.rem(q - step + ring, ring)
        came_r = lax.rem(q + step, ring)
        spare = right_send.at[0]

        @pl.when((side == 0) & (step < last))
        def _():
            chunk_copy(came_l, c, spare, recv.at[came_l, c], right).wait_recv()

            @pl.when(step < last - 1)
            def _():
                chunk_copy(came_l, c, right_send.at[step], recv.at[came_l, c], right).start()

            @pl.when(step == last - 1)
            def _():
                chunk_copy(came_l, c, right_send.at[step], half_recv.at[0], right, 0).start()

            chunk_copy(came_l, c, sib_send.at[b], recv.at[came_l, c], sibling).start()
            chunk_copy(came_r, c, spare, recv.at[came_r, c], left).wait_recv()

            @pl.when(step < last - 1)
            def _():
                chunk_copy(came_r, c, left_send.at[step], recv.at[came_r, c], left).start()

            @pl.when(step == last - 1)
            def _():
                chunk_copy(came_r, c, left_send.at[step], half_recv.at[1], left, 1).start()

            chunk_copy(came_r, c, sib_send.at[b + 1], recv.at[came_r, c], sibling).start()

        @pl.when(step == last)
        def _():
            chunk_copy(came_l, c, spare, half_recv.at[0], right, 0).wait_recv()
            chunk_copy(came_l, c, spare, half_recv.at[1], left, 1).wait_recv()
            chunk_copy(came_l, c, sib_send.at[b], recv.at[came_l, c], sibling).start()

        place = came_l + side * (came_r - came_l)
        chunk_copy(place, 1 - c, spare, recv.at[place, 1 - c], sibling).wait_recv()

        x = rows_buf[place].reshape(2 * rows, rows_buf.shape[3])
        target = jnp.concatenate([wanted_of(rank_of(place, 0)), wanted_of(rank_of(place, 1))], axis=1)
        target = target - r * vocab
        sub = lax.broadcasted_iota(jnp.int32, (8, 2 * rows), 0)
        peak = total = weighted = chosen = None
        for start, size in tiles:
            logits = lax.dot_general(
                table[pl.ds(start, size), :], x, (((1,), (1,)), ((), ())),
                preferred_element_type=jnp.float32,
            ).reshape(size // 8, 8, 2 * rows)
            line = lax.broadcasted_iota(jnp.int32, logits.shape, 0) * 8 + sub[None]
            if start + size > low_valid:
                logits = jnp.where(line < VREAL - r * vocab - start, logits, -1e30)
            hit = jnp.sum(jnp.where(line == target[None] - start, logits, 0.0), axis=0)
            top = jnp.max(logits, axis=0)
            new = top if peak is None else jnp.maximum(peak, top)
            diff = logits - new[None]
            weights = jnp.exp(diff)
            fresh_total = jnp.sum(weights, axis=0)
            fresh_weighted = jnp.sum(weights * diff, axis=0)
            if peak is None:
                total, weighted, chosen = fresh_total, fresh_weighted, hit
            else:
                move = peak - new
                factor = jnp.exp(move)
                weighted = factor * (weighted + total * move) + fresh_weighted
                total = factor * total + fresh_total
                chosen = chosen + hit
            peak = new
        top = jnp.max(peak, axis=0, keepdims=True)
        move = peak - top
        factor = jnp.exp(move)
        weighted = jnp.sum(factor * (weighted + total * move), axis=0, keepdims=True)
        total = jnp.sum(factor * total, axis=0, keepdims=True)
        chosen = jnp.sum(chosen, axis=0, keepdims=True)
        packed = jnp.concatenate([top, total, weighted, chosen, top, total, weighted, chosen], axis=0)
        fresh[place, 0] = packed[:, :rows]
        fresh[place, 1] = packed[:, rows:]

        for j in range(1, groups):
            stat_copy(b, place, 0, j).start()
            stat_copy(b, place, 1, j).start()

        @pl.when(b > 0)
        def _():
            stat_copy(b, place, 0, 0).start()
            stat_copy(b, place, 1, 0).start()

        @pl.when(b == 0)
        def _():
            stat_copy(b, place, 1 - c, 0).start()
            stats[0] = fresh[place, c]

        return carry

    lax.fori_loop(0, ring, block, 0)

    pltpu.make_async_remote_copy(
        src_ref=stats.at[others], dst_ref=stats.at[others], send_sem=ids_send.at[0],
        recv_sem=stat_recv, device_id=peer(1), device_id_type=MESH,
    ).wait_recv()

    for j in range(groups):
        peak = stats[j * n:(j + 1) * n, 0, :]
        total = stats[j * n:(j + 1) * n, 1, :]
        weighted = stats[j * n:(j + 1) * n, 2, :]
        chosen = jnp.sum(stats[j * n:(j + 1) * n, 3, :], axis=0, keepdims=True)
        top = jnp.max(peak, axis=0, keepdims=True)
        move = peak - top
        factor = jnp.exp(move)
        weighted = jnp.sum(factor * (weighted + total * move), axis=0, keepdims=True)
        total = jnp.sum(factor * total, axis=0, keepdims=True)
        log_total = jnp.log(total)
        out_ref[j] = jnp.concatenate([chosen - top - log_total, log_total - weighted / total], axis=0)

    def drain_ids(k, carry):
        ids_copy(k).wait_send()
        return carry

    lax.fori_loop(1, everyone, drain_ids, 0)

    def drain_ring(s, carry):
        chunk_copy(q, c, right_send.at[s], recv.at[q, c], right).wait_send()
        chunk_copy(q, c, left_send.at[s], recv.at[q, c], left).wait_send()
        return carry

    lax.fori_loop(0, last - 1, drain_ring, 0)
    chunk_copy(q, c, right_send.at[last - 1], recv.at[q, c], right, 0).wait_send()
    chunk_copy(q, c, left_send.at[last - 1], recv.at[q, c], left, 1).wait_send()

    def drain_block(b, carry):
        chunk_copy(q, c, sib_send.at[b], recv.at[q, c], sibling).wait_send()
        for j in range(1, groups):
            stat_copy(b, q, 0, j).wait_send()
            stat_copy(b, q, 1, j).wait_send()
        stat_copy(b, q, 1 - c, 0).wait_send()

        @pl.when(b > 0)
        def _():
            stat_copy(b, q, c, 0).wait_send()

        return carry

    lax.fori_loop(0, ring, drain_block, 0)


def local(groups, n, hidden, norm_gain, embedding, targets, lengths, loss_mask, deal_slots):
    seqs, width, depth = hidden.shape
    rows = seqs * width
    vocab = embedding.shape[0]
    ring = n // 2
    g = lax.axis_index("dp")
    r = lax.axis_index("tensor")
    every = jnp.arange(groups * seqs, dtype=jnp.int32)
    mine = g * seqs + jnp.arange(seqs, dtype=jnp.int32)
    order = jnp.sum(jnp.where(deal_slots[None, :] == mine[:, None], every[None, :], 0), axis=1)
    wanted = jnp.tile(targets, (1, seqs))
    dma = pltpu.SemaphoreType.DMA
    result = pl.pallas_call(
        functools.partial(
            kernel, groups, n, seqs, vocab_tiles(vocab, 528), VREAL - (n - 1) * vocab
        ),
        out_shape=jax.ShapeDtypeStruct((groups, 2, rows), jnp.float32),
        in_specs=[
            pl.BlockSpec(memory_space=pltpu.VMEM),
            pl.BlockSpec(memory_space=pltpu.VMEM),
            pl.BlockSpec(memory_space=pl.ANY),
            pl.BlockSpec(memory_space=pltpu.VMEM),
            pl.BlockSpec(memory_space=pltpu.SMEM),
        ],
        out_specs=pl.BlockSpec(memory_space=pltpu.VMEM),
        scratch_shapes=[
            pltpu.VMEM((ring, 2, rows, depth), jnp.bfloat16),
            pltpu.VMEM((vocab, depth), jnp.bfloat16),
            pltpu.VMEM((groups * n, seqs, rows), jnp.int32),
            pltpu.VMEM((ring, 2, 8, rows), jnp.float32),
            pltpu.VMEM((groups * n, 8, rows), jnp.float32),
            dma,
            dma((groups * n,)),
            dma,
            dma((ring // 2,)),
            dma((ring // 2,)),
            dma((ring,)),
            dma((ring, 2)),
            dma((2,)),
            dma((ring, 2, groups)),
            dma,
        ],
        compiler_params=pltpu.CompilerParams(
            collective_id=0, has_side_effects=True, vmem_limit_bytes=56 * 2**20
        ),
        cost_estimate=pl.CostEstimate(
            flops=2 * n * rows * vocab * depth,
            bytes_accessed=vocab * depth * 2,
            transcendentals=n * rows * vocab,
        ),
        name="ring_score",
    )(hidden.reshape(rows, depth), norm_gain.reshape(1, depth), embedding, wanted, order)
    slots = deal_slots[mine]
    back = lax.rem(g - slots // seqs + groups, groups)
    place = back * seqs + lax.rem(slots, seqs)
    pick = place[:, None] == jnp.arange(groups * seqs, dtype=jnp.int32)[None, :]
    flat = result.reshape(groups, 2, seqs, width).transpose(1, 0, 2, 3).reshape(2, groups * seqs, width)
    moved = jnp.sum(jnp.where(pick[None, :, :, None], flat[:, None], 0.0), axis=2)
    positions = r * width + jnp.arange(width, dtype=jnp.int32)
    scored = (positions[None, :] < lengths[mine][:, None]) & (loss_mask == 1)
    return jnp.where(scored, moved[0], 0.0), jnp.where(scored, moved[1], 0.0)


def solution(mesh):
    placed = (
        P("dp", "tensor", None),
        P(),
        P("tensor", None),
        P("dp", "tensor"),
        P(),
        P("dp", "tensor"),
        P(),
    )
    return jax.shard_map(
        functools.partial(local, mesh.shape["dp"], mesh.shape["tensor"]),
        mesh=mesh,
        in_specs=placed,
        out_specs=(P("dp", "tensor"), P("dp", "tensor")),
        check_vma=False,
    )
```

time: 230 us -> 74.2 us (0.32)
  blocking collectives: 112 us -> 0 us
  Pallas kernels: 0 us -> 65 us
  waiting for transfers between devices: 32.6 us -> 0 us
  matrix products: 26.9 us -> 0 us
  other arithmetic: 23.7 us -> 2.83 us
  between operations: 14.2 us -> 0.71 us
  starting transfers between devices: 10.7 us -> 0 us
  local copies, waits for them, and re-layouts: 9.65 us -> 5.36 us
    pallas_call x0 -> x1, Pallas kernels: none -> 65 us  [local(): pl.pallas_call(functools.partial(kernel, groups, n, seqs, vocab_tiles(voc...]
    psum x1 -> x0, blocking collectives: 57.6 us -> none  [score(): summed = lax.psum((totals * factor, weighted * factor, chosen), 'tensor')]
    pmax x1 -> x0, blocking collectives: 31.8 us -> none  [score(): overall = lax.pmax(maximum, 'tensor')]
    dot_general x1 -> x0, matrix products: 26.9 us -> none  [score(): jnp.einsum('nd,vd->nv', flat_rows, embedding, preferred_element_type=jnp....]
    all_gather x1 -> x0, waiting for transfers between devices: 26.9 us -> none  [score(): row_block = lax.all_gather(normed, 'tensor', axis=1, tiled=True)]
    all_gather x1 -> x0, blocking collectives: 22.5 us -> none  [score(): block_marks = lax.all_gather(marked, 'tensor', axis=1, tiled=True)]
    reduce_sum x2, other arithmetic: 15.9 us -> 1.46 us  [the longest x1 1.35 us: local(): jnp.sum(jnp.where(deal_slots[None, :] == mine[:, None], every[None, :], 0...]
    all_to_all x3 -> x0, starting transfers between devices: 10.7 us -> none  [the longest x1 4.23 us: local(): lax.all_to_all(marked[send_order], 'dp', split_axis=0, concat_axis=0, til...]
  transfers between devices with their start and end apart: 4 -> 0, of which waited for: 4 -> 0; matrix products, arithmetic and copies ran while one was open for 6% -> 0% of each run, Pallas kernels for 0% -> 0%
where the time goes in v1:
time: 74.2 us; the launch traced here: 73.9 us
  Pallas kernels  65 us (88%)
  local copies, waits for them, and re-layouts  5.36 us (7%)
  other arithmetic  2.83 us (4%)
    pallas_call x1, Pallas kernels, local(): pl.pallas_call(functools.partial(kernel, groups, n, seqs, vocab_tiles(voc...  65 us

profile of v1, /device:TPU:0, one launch (start us, length us, event | category | flops | bytes accessed | tf_op | source)
XLA Modules:
  0.0 73.9 jit_solution(12890399122116718399)
XLA Ops:
  0.6 0.0 copy-start
  0.7 1.3 %gather_fusion.1 = s32[8]{0:T(128)S(1)} fusion(s32[16]{0:T(128)} %param.13, s32[1024]{0:T(1024)S(1)} %pad_clamp_fusion), kind=kCustom, calls=%fused_computation.1 | custom fusion | bytes 96 | tf_op jit(solution)/shard_map/gather | solution.py:325
  2.0 0.1 iota_compare_fusion
  2.1 1.4 %select_reduce_fusion.1.order_ref = s32[8]{0:T(128)} fusion(s32[16]{0:T(128)} %param.13, s32[8]{0:T(128)S(1)} %iota_add_fusion), kind=kLoop, calls=%fused_computation.9 | loop fusion | flops 376 | bytes 128 | tf_op jit(solution)/shard_map/reduce_sum | solution.py:282
  3.4 0.7 tile.4
  4.1 0.7 tile.10.wanted_ref
  4.8 1.3 %reshape.92.gain_ref = f32[1,1536]{1,0:T(1,128)} reshape(f32[1536]{0:T(1024)} %param.8) | data formatting | bytes 12288 | tf_op jit(solution)/shard_map/reshape | solution.py:324
  6.1 0.0 copy-start.1
  6.1 65.0 %ring_score.1 = f32[2,2,128]{2,1,0:T(2,128)} custom-call(bf16[128,1536]{1,0:T(8,128)(2,1)} %bitcast.17, f32[1,1536]{1,0:T(1,128)} %reshape.92.gain_ref, bf16[3104,1536]{1,0:T(8,128)(2,1)} %table_hbm.1, s32[8,128]{1,0:T(8,128)} %tile.10.wanted_ref, s32[8]{0:T(128)} %select_reduce_fusion.1.order_ref), custom_call_target="tpu_custom_call" | custom-call | flops 19528679424 | bytes 9535488 | tf_op jit(solution)/shard_map/ring_score/pallas_call | solution.py:285
  71.1 0.7 %reshape.93 = f32[2,2,8,16]{3,2,1,0:T(8,128)S(1)} reshape(f32[2,2,128]{2,1,0:T(2,128)} %ring_score.1) | data formatting | bytes 4096 | tf_op jit(solution)/shard_map/reshape | solution.py:329
  71.9 0.1 select_reduce_fusion
  72.0 0.0 copy-done
  72.0 0.6 gather_fusion
  72.7 0.0 copy-done.1
  72.7 0.7 fusion
  73.4 0.6 fusion.1
  (6 shorter events, 0.0 us)
Async XLA Ops:
  0.6 71.4 %copy-start = (s32[16]{0:T(128)S(1)}, s32[16]{0:T(128)}, u32[]{:S(2)}) copy-start(s32[16]{0:T(128)} %param.11) | copy-start | bytes 196
  6.1 66.6 %copy-start.1 = (s32[8,16]{1,0:T(8,128)S(1)}, s32[8,16]{1,0:T(8,128)}, u32[]{:S(2)}) copy-start(s32[8,16]{1,0:T(8,128)} %param.12) | copy-start | bytes 1540

commit v2 on v1

--- a/solution.py
+++ b/solution.py
@@ -12,16 +12,16 @@
 
 
 def vocab_tiles(total, want):
-    units = -(-total // 16)
-    parts = max(1, -(-total // want))
-    starts = [16 * (units * i // parts) for i in range(parts)] + [total]
+    units = total // 32
+    parts = max(1, total // want)
+    starts = [32 * (units * i // parts) for i in range(parts)] + [total]
     return [(a, b - a) for a, b in zip(starts[:-1], starts[1:])]
 
 
 def kernel(
     groups, n, seqs, tiles, low_valid,
     hidden_ref, gain_ref, table_hbm, wanted_ref, order_ref, out_ref,
-    rows_buf, table, ids, fresh, stats,
+    rows_buf, table, ids, fresh, stats, logits,
     table_sem, ids_send, ids_recv, right_send, left_send, sib_send, recv, half_recv,
     stat_send, stat_recv,
 ):
@@ -67,7 +67,7 @@
 
     values = hidden_ref[...].astype(jnp.float32)
     inverse = lax.rsqrt(jnp.mean(values * values, axis=1, keepdims=True) + 1e-05)
-    rows_buf[q, c] = (values * inverse * gain_ref[...]).astype(jnp.bfloat16)
+    rows_buf[q, c] = (values * inverse * gain_ref[...][None, :]).astype(jnp.bfloat16)
     ids[0] = wanted_ref[...]
 
     pl.semaphore_wait(barrier, everyone - 1)
@@ -123,6 +123,43 @@
             device_id={"dp": lax.rem(g + j, groups), "tensor": rank}, device_id_type=MESH,
         )
 
+    def pass_on(b, step, side):
+        ahead = step + 1
+        next_l = lax.rem(q - ahead + ring, ring)
+        next_r = lax.rem(q + ahead, ring)
+        spare = right_send.at[0]
+
+        @pl.when((side == 1) & (ahead < last))
+        def _():
+            chunk_copy(next_l, c, spare, recv.at[next_l, c], right).wait_recv()
+
+            @pl.when(ahead < last - 1)
+            def _():
+                chunk_copy(next_l, c, right_send.at[ahead], recv.at[next_l, c], right).start()
+
+            @pl.when(ahead == last - 1)
+            def _():
+                chunk_copy(next_l, c, right_send.at[ahead], half_recv.at[0], right, 0).start()
+
+            chunk_copy(next_l, c, sib_send.at[b + 1], recv.at[next_l, c], sibling).start()
+            chunk_copy(next_r, c, spare, recv.at[next_r, c], left).wait_recv()
+
+            @pl.when(ahead < last - 1)
+            def _():
+                chunk_copy(next_r, c, left_send.at[ahead], recv.at[next_r, c], left).start()
+
+            @pl.when(ahead == last - 1)
+            def _():
+                chunk_copy(next_r, c, left_send.at[ahead], half_recv.at[1], left, 1).start()
+
+            chunk_copy(next_r, c, sib_send.at[b + 2], recv.at[next_r, c], sibling).start()
+
+        @pl.when((side == 1) & (ahead == last))
+        def _():
+            chunk_copy(next_l, c, spare, half_recv.at[0], right, 0).wait_recv()
+            chunk_copy(next_l, c, spare, half_recv.at[1], left, 1).wait_recv()
+            chunk_copy(next_l, c, sib_send.at[b + 1], recv.at[next_l, c], sibling).start()
+
     def block(b, carry):
         step = (b + 1) // 2
         side = lax.rem(b + 1, 2)
@@ -130,69 +167,67 @@
         came_r = lax.rem(q + step, ring)
         spare = right_send.at[0]
 
-        @pl.when((side == 0) & (step < last))
-        def _():
-            chunk_copy(came_l, c, spare, recv.at[came_l, c], right).wait_recv()
-
-            @pl.when(step < last - 1)
-            def _():
-                chunk_copy(came_l, c, right_send.at[step], recv.at[came_l, c], right).start()
-
-            @pl.when(step == last - 1)
-            def _():
-                chunk_copy(came_l, c, right_send.at[step], half_recv.at[0], right, 0).start()
-
-            chunk_copy(came_l, c, sib_send.at[b], recv.at[came_l, c], sibling).start()
-            chunk_copy(came_r, c, spare, recv.at[came_r, c], left).wait_recv()
-
-            @pl.when(step < last - 1)
-            def _():
-                chunk_copy(came_r, c, left_send.at[step], recv.at[came_r, c], left).start()
-
-            @pl.when(step == last - 1)
-            def _():
-                chunk_copy(came_r, c, left_send.at[step], half_recv.at[1], left, 1).start()
-
-            chunk_copy(came_r, c, sib_send.at[b + 1], recv.at[came_r, c], sibling).start()
-
-        @pl.when(step == last)
-        def _():
-            chunk_copy(came_l, c, spare, half_recv.at[0], right, 0).wait_recv()
-            chunk_copy(came_l, c, spare, half_recv.at[1], left, 1).wait_recv()
-            chunk_copy(came_l, c, sib_send.at[b], recv.at[came_l, c], sibling).start()
-
         place = came_l + side * (came_r - came_l)
         chunk_copy(place, 1 - c, spare, recv.at[place, 1 - c], sibling).wait_recv()
 
         x = rows_buf[place].reshape(2 * rows, rows_buf.shape[3])
         target = jnp.concatenate([wanted_of(rank_of(place, 0)), wanted_of(rank_of(place, 1))], axis=1)
-        target = target - r * vocab
         sub = lax.broadcasted_iota(jnp.int32, (8, 2 * rows), 0)
-        peak = total = weighted = chosen = None
-        for start, size in tiles:
-            logits = lax.dot_general(
+        target = target - r * vocab - sub
+        limit = VREAL - r * vocab - sub
+
+        def part(t, start, at, size):
+            piece = logits[t % 2, pl.ds(at, size), :].reshape(size // 8, 8, 2 * rows)
+            line = lax.broadcasted_iota(jnp.int32, piece.shape, 0) * 8 + (start + at)
+            if start + tiles[t][1] > low_valid:
+                piece = jnp.where(line < limit[None], piece, -1e30)
+            return piece, line
+
+        def sweep(size, step_at, state):
+            state = lax.fori_loop(
+                0, size // 32, lambda i, old: step_at(pl.multiple_of(i * 32, 32), 32, old), state,
+                unroll=True,
+            )
+            return step_at(size - size % 32, size % 32, state) if size % 32 else state
+
+        def add_tile(t, state):
+            start, size = tiles[t]
+            peak, total, weighted, chosen = state
+
+            def widen(at, many, new):
+                return jnp.maximum(new, jnp.max(part(t, start, at, many)[0], axis=0))
+
+            new = sweep(size, widen, peak)
+            move = peak - new
+            factor = jnp.exp(move)
+            weighted = factor * (weighted + total * move)
+            total = factor * total
+
+            def add(at, many, old):
+                total, weighted, chosen = old
+                piece, line = part(t, start, at, many)
+                diff = piece - new[None]
+                weights = jnp.exp(diff)
+                total = total + jnp.sum(weights, axis=0)
+                weighted = weighted + jnp.sum(weights * diff, axis=0)
+                chosen = chosen + jnp.sum(jnp.where(line == target[None], piece, 0.0), axis=0)
+                return total, weighted, chosen
+
+            total, weighted, chosen = sweep(size, add, (total, weighted, chosen))
+            return new, total, weighted, chosen
+
+        zero = jnp.zeros((8, 2 * rows), jnp.float32)
+        state = (zero - 1e30, zero, zero, zero)
+        for t, (start, size) in enumerate(tiles):
+            if t == len(tiles) // 2:
+                pass_on(b, step, side)
+            logits[t % 2, :size, :] = lax.dot_general(
                 table[pl.ds(start, size), :], x, (((1,), (1,)), ((), ())),
                 preferred_element_type=jnp.float32,
-            ).reshape(size // 8, 8, 2 * rows)
-            line = lax.broadcasted_iota(jnp.int32, logits.shape, 0) * 8 + sub[None]
-            if start + size > low_valid:
-                logits = jnp.where(line < VREAL - r * vocab - start, logits, -1e30)
-            hit = jnp.sum(jnp.where(line == target[None] - start, logits, 0.0), axis=0)
-            top = jnp.max(logits, axis=0)
-            new = top if peak is None else jnp.maximum(peak, top)
-            diff = logits - new[None]
-            weights = jnp.exp(diff)
-            fresh_total = jnp.sum(weights, axis=0)
-            fresh_weighted = jnp.sum(weights * diff, axis=0)
-            if peak is None:
-                total, weighted, chosen = fresh_total, fresh_weighted, hit
-            else:
-                move = peak - new
-                factor = jnp.exp(move)
-                weighted = factor * (weighted + total * move) + fresh_weighted
-                total = factor * total + fresh_total
-                chosen = chosen + hit
-            peak = new
+            )
+            if t:
+                state = add_tile(t - 1, state)
+        peak, total, weighted, chosen = add_tile(len(tiles) - 1, state)
         top = jnp.max(peak, axis=0, keepdims=True)
         move = peak - top
         factor = jnp.exp(move)
@@ -280,11 +315,12 @@
     every = jnp.arange(groups * seqs, dtype=jnp.int32)
     mine = g * seqs + jnp.arange(seqs, dtype=jnp.int32)
     order = jnp.sum(jnp.where(deal_slots[None, :] == mine[:, None], every[None, :], 0), axis=1)
-    wanted = jnp.tile(targets, (1, seqs))
+    wanted = jnp.concatenate([targets] * seqs, axis=1)
+    tiles = vocab_tiles(vocab, 512)
     dma = pltpu.SemaphoreType.DMA
     result = pl.pallas_call(
         functools.partial(
-            kernel, groups, n, seqs, vocab_tiles(vocab, 528), VREAL - (n - 1) * vocab
+            kernel, groups, n, seqs, tiles, VREAL - (n - 1) * vocab
         ),
         out_shape=jax.ShapeDtypeStruct((groups, 2, rows), jnp.float32),
         in_specs=[
@@ -301,6 +337,7 @@
             pltpu.VMEM((groups * n, seqs, rows), jnp.int32),
             pltpu.VMEM((ring, 2, 8, rows), jnp.float32),
             pltpu.VMEM((groups * n, 8, rows), jnp.float32),
+            pltpu.VMEM((2, max(size for _, size in tiles), 2 * rows), jnp.float32),
             dma,
             dma((groups * n,)),
             dma,
@@ -321,15 +358,15 @@
             transcendentals=n * rows * vocab,
         ),
         name="ring_score",
-    )(hidden.reshape(rows, depth), norm_gain.reshape(1, depth), embedding, wanted, order)
-    slots = deal_slots[mine]
+    )(hidden.reshape(rows, depth), norm_gain, embedding, wanted, order)
+    slots = lax.dynamic_slice_in_dim(deal_slots, g * seqs, seqs)
     back = lax.rem(g - slots // seqs + groups, groups)
     place = back * seqs + lax.rem(slots, seqs)
     pick = place[:, None] == jnp.arange(groups * seqs, dtype=jnp.int32)[None, :]
     flat = result.reshape(groups, 2, seqs, width).transpose(1, 0, 2, 3).reshape(2, groups * seqs, width)
     moved = jnp.sum(jnp.where(pick[None, :, :, None], flat[:, None], 0.0), axis=2)
     positions = r * width + jnp.arange(width, dtype=jnp.int32)
-    scored = (positions[None, :] < lengths[mine][:, None]) & (loss_mask == 1)
+    scored = (positions[None, :] < lax.dynamic_slice_in_dim(lengths, g * seqs, seqs)[:, None]) & (loss_mask == 1)
     return jnp.where(scored, moved[0], 0.0), jnp.where(scored, moved[1], 0.0)
 
 

time: 74.2 us -> 72 us (0.970)
  local copies, waits for them, and re-layouts: 5.36 us -> 2.5 us
    gather x2 -> x0, local copies, waits for them, and re-layouts: 1.94 us -> none  [the longest x1 1.3 us: local(): slots = deal_slots[mine]]
    concatenate x0 -> x1, local copies, waits for them, and re-layouts: none -> 1.65 us  [local(): wanted = jnp.concatenate([targets] * seqs, axis=1)]
    another operation x2 -> x0, local copies, waits for them, and re-layouts: 1.36 us -> none  [local(): wanted = jnp.tile(targets, (1, seqs))]
    reshape x1 -> x0, local copies, waits for them, and re-layouts: 1.3 us -> none  [local(): norm_gain.reshape(1, depth)]
where the time goes in v2:
time: 72 us; the launch traced here: 71.8 us
  Pallas kernels  65.7 us (91%)
  other arithmetic  2.88 us (4%)
  local copies, waits for them, and re-layouts  2.5 us (3%)
    pallas_call x1, Pallas kernels, local(): pl.pallas_call(functools.partial(kernel, groups, n, seqs, tiles, VREAL -...  65.7 us
    concatenate x1, local copies, waits for them, and re-layouts, local(): wanted = jnp.concatenate([targets] * seqs, axis=1)  1.65 us

profile of v2, /device:TPU:0, one launch (start us, length us, event | category | flops | bytes accessed | tf_op | source)
XLA Modules:
  0.0 71.8 jit_solution(15064573794084441577)
XLA Ops:
  0.6 1.6 %concatenate.3.wanted_ref = s32[8,128]{1,0:T(8,128)} concatenate(s32[8,16]{1,0:T(8,128)} %param.10, s32[8,16]{1,0:T(8,128)} %param.10, s32[8,16]{1,0:T(8,128)} %param.10, s32[8,16]{1,0:T(8,128)} %param.10, s32[8,16]{1,0:T(8,128)} %param.10, s32[8,16]{1,0:T(8,128)} %param.10, s32[8,16]{1,0:T(8,128)} %param.10, s32[8,16]{1,0:T(8,128)} %param.10), dimensions={1} | concatenate | bytes 8192 | tf_op jit(solution)/shard_map/concatenate | solution.py:318
  2.3 1.3 %select_reduce_fusion.1.order_ref = s32[8]{0:T(128)} fusion(s32[16]{0:T(128)} %param.13, s32[8]{0:T(128)S(1)} %iota_add_fusion), kind=kLoop, calls=%fused_computation.6 | loop fusion | flops 376 | bytes 128 | tf_op jit(solution)/shard_map/reduce_sum | solution.py:317
  3.6 0.0 copy-start.1
  3.6 0.0 copy-start.2
  3.6 0.0 copy-start
  3.6 65.7 %ring_score.1 = f32[2,2,128]{2,1,0:T(2,128)} custom-call(bf16[128,1536]{1,0:T(8,128)(2,1)} %bitcast.15, f32[1536]{0:T(1024)} %gain_ref.1, bf16[3104,1536]{1,0:T(8,128)(2,1)} %table_hbm.1, s32[8,128]{1,0:T(8,128)} %concatenate.3.wanted_ref, s32[8]{0:T(128)} %select_reduce_fusion.1.order_ref), custom_call_target="tpu_custom_call" | custom-call | flops 19528679424 | bytes 9535488 | tf_op jit(solution)/shard_map/ring_score/pallas_call | solution.py:321
  69.4 0.8 %reshape.43 = f32[2,2,8,16]{3,2,1,0:T(8,128)S(1)} reshape(f32[2,2,128]{2,1,0:T(2,128)} %ring_score.1) | data formatting | bytes 4096 | tf_op jit(solution)/shard_map/reshape | solution.py:366
  70.1 0.0 copy-done.1
  70.1 0.1 fusion.4
  70.2 0.1 iota_compare_fusion
  70.3 0.1 select_reduce_fusion
  70.4 0.0 copy-done.2
  70.4 0.1 dynamic_slice.6
  70.5 0.0 copy-done
  70.5 0.7 fusion
  71.2 0.6 fusion.1
  (3 shorter events, 0.0 us)
Async XLA Ops:
  3.6 66.5 %copy-start.1 = (s32[16]{0:T(128)S(1)}, s32[16]{0:T(128)}, u32[]{:S(2)}) copy-start(s32[16]{0:T(128)} %param.13) | copy-start | bytes 196
  3.6 66.8 %copy-start.2 = (s32[16]{0:T(128)S(1)}, s32[16]{0:T(128)}, u32[]{:S(2)}) copy-start(s32[16]{0:T(128)} %param.11) | copy-start | bytes 196
  3.6 66.9 %copy-start = (s32[8,16]{1,0:T(8,128)S(1)}, s32[8,16]{1,0:T(8,128)}, u32[]{:S(2)}) copy-start(s32[8,16]{1,0:T(8,128)} %param.12) | copy-start | bytes 1540

commit v3 on v2

--- a/solution.py
+++ b/solution.py
@@ -170,7 +170,7 @@
         place = came_l + side * (came_r - came_l)
         chunk_copy(place, 1 - c, spare, recv.at[place, 1 - c], sibling).wait_recv()
 
-        x = rows_buf[place].reshape(2 * rows, rows_buf.shape[3])
+        x = rows_buf[place].reshape(2 * rows, rows_buf.shape[3]).T
         target = jnp.concatenate([wanted_of(rank_of(place, 0)), wanted_of(rank_of(place, 1))], axis=1)
         sub = lax.broadcasted_iota(jnp.int32, (8, 2 * rows), 0)
         target = target - r * vocab - sub
@@ -222,7 +222,7 @@
             if t == len(tiles) // 2:
                 pass_on(b, step, side)
             logits[t % 2, :size, :] = lax.dot_general(
-                table[pl.ds(start, size), :], x, (((1,), (1,)), ((), ())),
+                table[pl.ds(start, size), :], x, (((1,), (0,)), ((), ())),
                 preferred_element_type=jnp.float32,
             )
             if t:
@@ -315,7 +315,7 @@
     every = jnp.arange(groups * seqs, dtype=jnp.int32)
     mine = g * seqs + jnp.arange(seqs, dtype=jnp.int32)
     order = jnp.sum(jnp.where(deal_slots[None, :] == mine[:, None], every[None, :], 0), axis=1)
-    wanted = jnp.concatenate([targets] * seqs, axis=1)
+    wanted = jnp.tile(targets, (1, seqs))
     tiles = vocab_tiles(vocab, 512)
     dma = pltpu.SemaphoreType.DMA
     result = pl.pallas_call(

time: 72 us -> 71.6 us (level)
    concatenate x1 -> x0, local copies, waits for them, and re-layouts: 1.65 us -> none  [local(): wanted = jnp.concatenate([targets] * seqs, axis=1)]
    another operation x0 -> x2, local copies, waits for them, and re-layouts: none -> 1.36 us  [local(): wanted = jnp.tile(targets, (1, seqs))]
where the time goes in v3:
time: 71.6 us; the launch traced here: 71.4 us
  Pallas kernels  65.7 us (92%)
  other arithmetic  2.88 us (4%)
  local copies, waits for them, and re-layouts  2.22 us (3%)
    pallas_call x1, Pallas kernels, local(): pl.pallas_call(functools.partial(kernel, groups, n, seqs, tiles, VREAL -...  65.7 us

profile of v3, /device:TPU:0, one launch (start us, length us, event | category | flops | bytes accessed | tf_op | source)
XLA Modules:
  0.0 71.4 jit_solution(14288035486081431733)
XLA Ops:
  0.6 0.7 tile.4
  1.3 0.7 tile.10.wanted_ref
  2.0 1.3 %select_reduce_fusion.1.order_ref = s32[8]{0:T(128)} fusion(s32[16]{0:T(128)} %param.13, s32[8]{0:T(128)S(1)} %iota_add_fusion), kind=kLoop, calls=%fused_computation.6 | loop fusion | flops 376 | bytes 128 | tf_op jit(solution)/shard_map/reduce_sum | solution.py:317
  3.3 0.0 copy-start.1
  3.3 0.0 copy-start.2
  3.3 0.0 copy-start
  3.3 65.7 %ring_score.1 = f32[2,2,128]{2,1,0:T(2,128)} custom-call(bf16[128,1536]{1,0:T(8,128)(2,1)} %bitcast.15, f32[1536]{0:T(1024)} %gain_ref.1, bf16[3104,1536]{1,0:T(8,128)(2,1)} %table_hbm.1, s32[8,128]{1,0:T(8,128)} %tile.10.wanted_ref, s32[8]{0:T(128)} %select_reduce_fusion.1.order_ref), custom_call_target="tpu_custom_call" | custom-call | flops 19528679424 | bytes 9535488 | tf_op jit(solution)/shard_map/ring_score/pallas_call | solution.py:321
  69.0 0.8 %reshape.47 = f32[2,2,8,16]{3,2,1,0:T(8,128)S(1)} reshape(f32[2,2,128]{2,1,0:T(2,128)} %ring_score.1) | data formatting | bytes 4096 | tf_op jit(solution)/shard_map/reshape | solution.py:366
  69.8 0.0 copy-done.1
  69.8 0.1 fusion.4
  69.9 0.1 iota_compare_fusion
  70.0 0.1 select_reduce_fusion
  70.1 0.0 copy-done.2
  70.1 0.1 dynamic_slice.6
  70.2 0.0 copy-done
  70.2 0.7 fusion
  70.8 0.6 fusion.1
  (3 shorter events, 0.0 us)
Async XLA Ops:
  3.3 66.5 %copy-start.1 = (s32[16]{0:T(128)S(1)}, s32[16]{0:T(128)}, u32[]{:S(2)}) copy-start(s32[16]{0:T(128)} %param.13) | copy-start | bytes 196
  3.3 66.7 %copy-start.2 = (s32[16]{0:T(128)S(1)}, s32[16]{0:T(128)}, u32[]{:S(2)}) copy-start(s32[16]{0:T(128)} %param.11) | copy-start | bytes 196
  3.3 66.8 %copy-start = (s32[8,16]{1,0:T(8,128)S(1)}, s32[8,16]{1,0:T(8,128)}, u32[]{:S(2)}) copy-start(s32[8,16]{1,0:T(8,128)} %param.12) | copy-start | bytes 1540
